TPU v7x, 32 devices: a whole 2x2x4 slice. The times are simulated.
32 devices in a mesh: section: 4 (over x, core), ctx: 2 (over y), tp: 4 (over z).
Axes of the slice: x: 2, y: 2, z: 4, core: 2. Of those that a mesh axis runs over, the one named last changes fastest.
Arguments:
- mixer_input: bfloat16 [4, 1024, 8192], P('section', 'ctx', 'tp'), may hold values from -6 to 6
- write_vectors: bfloat16 [4, 1024, 1024], P('section', 'ctx', 'tp'), may hold values from -6 to 6
- read_vectors: bfloat16 [4, 1024, 1024], P('section', 'ctx', 'tp'), may hold values from -6 to 6
- delta_raw: float32 [4, 1024, 128], P('section', 'ctx', 'tp'), as said below
- log_rates: float32 [4, 128], P('section', 'tp'), as said below
- delta_bias: float32 [4, 128], P('section', 'tp'), as said below
- skip_gain: float32 [4, 128], P('section', 'tp'), may hold values from 0.5 to 1.5
- output_grad: bfloat16 [4, 1024, 8192], P('section', 'ctx', 'tp'), may hold values from -6 to 6
Outputs:
- upstream_grad: bfloat16 [4, 1024, 8192], P('section', 'ctx', 'tp')
- grad_delta: float32 [4, 1024, 128], P('section', 'ctx', 'tp')
- grad_vectors: float32 [4, 1024, 2048], P('section', ('ctx', 'tp'))
- grad_params: float32 [4, 3, 128], P('section', None, 'tp')
Inputs may be any that keep to these rules, and one draw needn't show every extreme that they name: `log_rates`: one value a head and section. `delta_bias`: one value a head and section. `delta_raw`: real-valued logits.
All inputs are finite; a program needn't handle non-finite values.
Results may differ from a plain program's by a relative error of at most 0.00365.
Values may be sent and summed in bfloat16 or wider, within the bound.
A program may use at most 128 MiB of HBM per device.

v0:
```python
import functools
import math

import jax
import jax.numpy as jnp
from jax import lax
from jax.experimental import pallas as pl
from jax.experimental.pallas import tpu as pltpu
from jax.sharding import PartitionSpec as P

HEADDIM = 64
STATE = 128
LANES = 128
LOG2E = math.log2(math.e)
MESH = pl.DeviceIdType.MESH
HIGHEST = lax.Precision.HIGHEST
F32 = jnp.float32
BF16 = jnp.bfloat16


def dot_nn(a, b, precision=None):
    return lax.dot_general(
        a, b, (((1,), (0,)), ((), ())), precision=precision, preferred_element_type=F32
    )


def dot_nt(a, b):
    return lax.dot_general(a, b, (((1,), (1,)), ((), ())), preferred_element_type=F32)


def dot_tn(a, b):
    return lax.dot_general(a, b, (((0,), (0,)), ((), ())), preferred_element_type=F32)


def kernel(
    sizes,
    x_ref,
    w_ref,
    r_ref,
    delta_ref,
    rates_ref,
    bias_ref,
    skip_ref,
    dy_ref,
    up_ref,
    gdelta_ref,
    vec_ref,
    params_ref,
    cum,
    cum_rows,
    step_rows,
    tail,
    decay,
    ratio,
    slope,
    lead_wide,
    tail_wide,
    lead_dy,
    tail_x,
    states,
    exits,
    state_in,
    state_out,
    exit_in,
    exit_out,
    read_state,
    write_exit,
    da,
    pieces,
    edge,
    dx,
    vec_out,
    vec_in,
    part,
    parts,
    s_send,
    s_recv,
    e_send,
    e_recv,
    x_send,
    x_recv,
    v_send,
    v_recv,
    p_send,
    p_recv,
):
    sections, ctxs, tps = sizes
    section, ctx, tp = (lax.axis_index(a) for a in ("section", "ctx", "tp"))
    length, heads = delta_ref.shape
    groups = w_ref.shape[1] // STATE
    per_group = heads // groups
    width = per_group * HEADDIM
    chunk = length // tps
    chunks = tps
    pairs = width // LANES

    barrier = pltpu.get_barrier_semaphore()
    for hop in range(1, ctxs):
        pl.semaphore_signal(
            barrier, inc=1, device_id={"ctx": lax.rem(ctx + hop, ctxs)}, device_id_type=MESH
        )
    for hop in range(1, tps):
        pl.semaphore_signal(
            barrier, inc=1, device_id={"tp": lax.rem(tp + hop, tps)}, device_id_type=MESH
        )

    @pl.when(section > 0)
    def _():
        pl.semaphore_signal(barrier, inc=1, device_id={"section": section - 1}, device_id_type=MESH)

    @pl.when(section < sections - 1)
    def _():
        pl.semaphore_signal(barrier, inc=1, device_id={"section": section + 1}, device_id_type=MESH)

    up_to = lax.broadcasted_iota(jnp.int32, (chunk, chunk), 0)
    from_ = lax.broadcasted_iota(jnp.int32, (chunk, chunk), 1)
    causal = up_to >= from_
    lower = causal.astype(F32)
    upper = (up_to <= from_).astype(F32)
    first_half = lax.broadcasted_iota(jnp.int32, (chunk, LANES), 1) < HEADDIM
    rate = jnp.exp(rates_ref[...])
    for k in range(chunks):
        rows = slice(k * chunk, (k + 1) * chunk)
        z = delta_ref[rows, :] + bias_ref[...]
        small = jnp.exp(-jnp.abs(z))
        step = jnp.maximum(z, 0.0) + jnp.log1p(small)
        sig = jnp.where(z >= 0, 1.0, small) / (1.0 + small)
        dec = -step * rate
        decay[rows, :] = dec
        ratio[rows, :] = jnp.where(step > 1e-37, sig / jnp.maximum(step, 1e-37), 1.0)
        slope[rows, :] = sig * rate
        run = dot_nn(lower, dec * LOG2E, HIGHEST)
        cum[rows, :] = run
        tail[rows, :] = jnp.exp2(run[chunk - 1 : chunk, :] - run) * step
        cum_rows[:, rows] = jnp.transpose(run)
        step_rows[:, rows] = jnp.transpose(step)

    def entered():
        peers = (ctxs - 1) + (tps - 1)
        peers = peers + jnp.where(section > 0, 1, 0) + jnp.where(section < sections - 1, 1, 0)
        pl.semaphore_wait(barrier, peers)

    def columns(g, j):
        start = g * width + j * LANES
        return slice(start, start + LANES)

    def spread(ref, rows, head):
        both = ref[rows, head : head + 2]
        return jnp.where(
            first_half,
            jnp.broadcast_to(both[:, 0:1], (chunk, LANES)),
            jnp.broadcast_to(both[:, 1:2], (chunk, LANES)),
        )

    def increments(g):
        def one(k, carry):
            rows = pl.ds(pl.multiple_of(k * chunk, chunk), chunk)
            for j in range(pairs):
                at = columns(g, j)
                head = g * per_group + 2 * j
                lead_pair = jnp.exp2(spread(cum, rows, head))
                tail_pair = spread(tail, rows, head)
                lead_wide[rows, at] = lead_pair
                tail_wide[rows, at] = tail_pair
                lead_dy[rows, at] = (lead_pair * dy_ref[rows, at].astype(F32)).astype(BF16)
                tail_x[rows, at] = (tail_pair * x_ref[rows, at].astype(F32)).astype(BF16)
            group_at = slice(g * width, (g + 1) * width)
            vec_at = slice(g * STATE, (g + 1) * STATE)
            states[g, k] = dot_tn(w_ref[rows, vec_at], tail_x[rows, group_at])
            exits[g, k] = dot_tn(r_ref[rows, vec_at], lead_dy[rows, group_at])
            return carry

        lax.fori_loop(0, chunks, one, 0)

    def last_row(g, k, j):
        row = (k + 1) * chunk - 1
        return lead_wide[row : row + 1, columns(g, j)]

    def scan_states(g, first):
        for j in range(pairs):
            at = slice(j * LANES, (j + 1) * LANES)
            now = jnp.zeros((STATE, LANES), F32) if first else state_in[g, :, at].astype(F32)
            for k in range(chunks):
                new = states[g, k, :, at]
                states[g, k, :, at] = now
                now = last_row(g, k, j) * now + new
            states[g, chunks, :, at] = now
            state_out[g, :, at] = now.astype(BF16)

    def scan_exits(g, first):
        for j in range(pairs):
            at = slice(j * LANES, (j + 1) * LANES)
            now = jnp.zeros((STATE, LANES), F32) if first else exit_in[g, :, at].astype(F32)
            for k in reversed(range(chunks)):
                new = exits[g, k, :, at]
                exits[g, k, :, at] = now
                now = last_row(g, k, j) * now + new
            exit_out[g, :, at] = now.astype(BF16)

    def state_copy(g):
        return pltpu.make_async_remote_copy(
            src_ref=state_out.at[g],
            dst_ref=state_in.at[g],
            send_sem=s_send.at[g],
            recv_sem=s_recv.at[g],
            device_id={"ctx": jnp.minimum(ctx + 1, ctxs - 1)},
            device_id_type=MESH,
        )

    def exit_copy(g):
        return pltpu.make_async_remote_copy(
            src_ref=exit_out.at[g],
            dst_ref=exit_in.at[g],
            send_sem=e_send.at[g],
            recv_sem=e_recv.at[g],
            device_id={"ctx": jnp.maximum(ctx - 1, 0)},
            device_id_type=MESH,
        )

    def begin(g):
        @pl.when(ctx == 0)
        def _():
            scan_states(g, True)
            if ctxs > 1:
                state_copy(g).start()

        @pl.when(ctx == ctxs - 1)
        def _():
            scan_exits(g, True)
            if ctxs > 1:
                exit_copy(g).start()

    def link(g):
        @pl.when(ctx > 0)
        def _():
            state_copy(g).wait_recv()
            scan_states(g, False)

        if ctxs > 2:

            @pl.when((ctx > 0) & (ctx < ctxs - 1))
            def _():
                state_copy(g).start()

        @pl.when(ctx < ctxs - 1)
        def _():
            exit_copy(g).wait_recv()
            scan_exits(g, False)

        if ctxs > 2:

            @pl.when((ctx > 0) & (ctx < ctxs - 1))
            def _():
                exit_copy(g).start()

    def dx_copy(g, k):
        rows = pl.ds(pl.multiple_of(k * chunk, chunk), chunk)
        at = pl.ds(g * width, width)
        return pltpu.make_async_remote_copy(
            src_ref=dx.at[rows, at],
            dst_ref=up_ref.at[rows, at],
            send_sem=x_send.at[g, k],
            recv_sem=x_recv.at[g, k],
            device_id={"section": jnp.maximum(section - 1, 0)},
            device_id_type=MESH,
        )

    def vec_copy(g, k):
        return pltpu.make_async_remote_copy(
            src_ref=vec_out.at[g, k],
            dst_ref=vec_in.at[g, tp],
            send_sem=v_send.at[g, k],
            recv_sem=v_recv.at[g, tp],
            device_id={"tp": k},
            device_id_type=MESH,
        )

    def vec_arrival(g, k):
        return pltpu.make_async_remote_copy(
            src_ref=vec_out.at[g, k],
            dst_ref=vec_in.at[g, k],
            send_sem=v_send.at[g, k],
            recv_sem=v_recv.at[g, k],
            device_id={"tp": k},
            device_id_type=MESH,
        )

    def quadratic(g):
        vec_at = slice(g * STATE, (g + 1) * STATE)
        group_at = slice(g * width, (g + 1) * width)
        gather = (
            lax.broadcasted_iota(jnp.int32, (width, heads), 0) // HEADDIM + g * per_group
            == lax.broadcasted_iota(jnp.int32, (width, heads), 1)
        ).astype(F32)
        gather_short = gather.astype(BF16)

        def one(k, carry):
            rows = pl.ds(pl.multiple_of(k * chunk, chunk), chunk)
            w, r = w_ref[rows, vec_at], r_ref[rows, vec_at]
            scores = jnp.where(causal, dot_nt(r, w), 0.0)
            da[...] = jnp.zeros_like(da)
            state, exit_ = states[g, k].astype(BF16), exits[g, k].astype(BF16)
            read_state[...] = dot_nn(r, state)
            write_exit[...] = dot_nn(w, exit_)
            edge[0:1, :] = jnp.sum(exits[g, k] * states[g, k + 1], axis=0, keepdims=True)
            for j in range(pairs):
                at = columns(g, j)
                here = slice(j * LANES, (j + 1) * LANES)
                head = g * per_group + 2 * j
                xs, dys = x_ref[rows, at], dy_ref[rows, at]
                none = jnp.zeros_like(xs)
                x_split = jnp.concatenate(
                    [jnp.where(first_half, xs, none), jnp.where(first_half, none, xs)], axis=0
                )
                dy_split = jnp.concatenate(
                    [jnp.where(first_half, dys, none), jnp.where(first_half, none, dys)], axis=0
                )
                product = dot_nt(dy_split, xs)
                weights = []
                total = da[...]
                for u in range(2):
                    one_head = head + u
                    gap = cum[rows, one_head : one_head + 1] - cum_rows[one_head : one_head + 1, rows]
                    kept = jnp.exp2(jnp.minimum(gap, 0.0)) * step_rows[one_head : one_head + 1, rows]
                    weights.append((kept * scores).astype(BF16))
                    total = total + kept * product[u * chunk : (u + 1) * chunk]
                da[...] = total
                y = dot_nn(jnp.concatenate(weights, axis=1), x_split)
                y = y + lead_wide[rows, at] * read_state[:, here]
                dxs = dot_tn(jnp.concatenate(weights, axis=0), dy_split)
                dxs = dxs + tail_wide[rows, at] * write_exit[:, here]
                x32, dy32 = xs.astype(F32), dys.astype(F32)
                column = x32 * dxs
                rest = dy32 * y - column
                high = rest.astype(BF16)
                pieces[0:chunk, here] = high
                pieces[chunk : 2 * chunk, here] = (rest - high.astype(F32)).astype(BF16)
                pieces[2 * chunk : 3 * chunk, here] = column.astype(BF16)
                edge[1:2, here] = jnp.sum(x32 * dy32, axis=0, keepdims=True)
                gain = jnp.where(
                    first_half[0:1],
                    jnp.broadcast_to(skip_ref[:, head : head + 1], (1, LANES)),
                    jnp.broadcast_to(skip_ref[:, head + 1 : head + 2], (1, LANES)),
                )
                dx[rows, at] = (dxs + gain * dy32).astype(BF16)

            @pl.when(section > 0)
            def _():
                dx_copy(g, k).start()

            inner = jnp.where(causal, da[...], 0.0).astype(BF16)
            dw = dot_tn(inner, r) + dot_nt(tail_x[rows, group_at], exit_)
            dr = dot_nn(inner, w) + dot_nt(lead_dy[rows, group_at], state)

            @pl.when(tp == k)
            def _():
                vec_in[g, k, :, 0:STATE] = dw.astype(BF16)
                vec_in[g, k, :, STATE : 2 * STATE] = dr.astype(BF16)

            @pl.when(tp != k)
            def _():
                vec_out[g, k, :, 0:STATE] = dw.astype(BF16)
                vec_out[g, k, :, STATE : 2 * STATE] = dr.astype(BF16)
                vec_copy(g, k).start()

            sums = dot_nn(pieces[...], gather_short)
            ends = dot_nn(edge[...], gather, HIGHEST)
            difference = sums[0:chunk] + sums[chunk : 2 * chunk]
            decay_grad = dot_nn(upper, difference, HIGHEST) + ends[0:1]
            grad = sums[2 * chunk : 3 * chunk] * ratio[rows, :] - decay_grad * slope[rows, :]
            mine = lax.broadcasted_iota(jnp.int32, (chunk, heads), 1) // per_group == g
            grad = jnp.where(mine, grad, 0.0)
            if g == 0:
                gdelta_ref[rows, :] = grad
            else:
                gdelta_ref[rows, :] += grad
            part[0:1, 0:heads] += jnp.sum(decay_grad * decay[rows, :], axis=0, keepdims=True)
            part[1:2, 0:heads] += jnp.sum(grad, axis=0, keepdims=True)
            part[2:3, 0:heads] += ends[1:2]
            return carry

        lax.fori_loop(0, chunks, one, 0)

    part[...] = jnp.zeros_like(part)
    edge[...] = jnp.zeros_like(edge)
    for g in range(groups):
        increments(g)
        if g == 0:
            entered()
        begin(g)
    for g in range(groups):
        link(g)
        quadratic(g)

    def part_copy(hop):
        other = lax.rem(ctx + hop, ctxs)
        return pltpu.make_async_remote_copy(
            src_ref=part,
            dst_ref=parts.at[hop - 1],
            send_sem=p_send.at[hop - 1],
            recv_sem=p_recv.at[hop - 1],
            device_id={"ctx": other},
            device_id_type=MESH,
        )

    for hop in range(1, ctxs):
        part_copy(hop).start()
    for g in range(groups):

        @pl.when(ctx < ctxs - 1)
        def _():
            state_copy(g).wait_send()

        @pl.when(ctx > 0)
        def _():
            exit_copy(g).wait_send()

        def vectors(k, carry):
            @pl.when(tp != k)
            def _():
                vec_arrival(g, k).wait_recv()
                vec_arrival(g, k).wait_send()

            return carry

        lax.fori_loop(0, tps, vectors, 0)
        for k in range(tps):
            start = (k * groups + g) * 2 * STATE
            vec_ref[:, start : start + 2 * STATE] = vec_in[g, k].astype(F32)
    result = part[...]
    for hop in range(1, ctxs):
        part_copy(hop).wait()
        result = result + parts[hop - 1]
    params_ref[...] = result[0:3, 0:heads]
    for g in range(groups):

        def moved(k, carry):
            @pl.when(section > 0)
            def _():
                dx_copy(g, k).wait_send()

            @pl.when(section < sections - 1)
            def _():
                dx_copy(g, k).wait_recv()

            return carry

        lax.fori_loop(0, chunks, moved, 0)


def shards(
    sizes,
    mixer_input,
    write_vectors,
    read_vectors,
    delta_raw,
    log_rates,
    delta_bias,
    skip_gain,
    output_grad,
):
    sections, ctxs, tps = sizes
    length, heads = delta_raw.shape[1:]
    columns = mixer_input.shape[2]
    groups = write_vectors.shape[2] // STATE
    width = columns // groups
    chunk = length // tps
    dma = pltpu.SemaphoreType.DMA
    vmem = pltpu.VMEM
    scratch = [
        vmem((length, heads), F32),
        vmem((heads, length), F32),
        vmem((heads, length), F32),
        vmem((length, heads), F32),
        vmem((length, heads), F32),
        vmem((length, heads), F32),
        vmem((length, heads), F32),
        vmem((length, columns), F32),
        vmem((length, columns), F32),
        vmem((length, columns), BF16),
        vmem((length, columns), BF16),
        vmem((groups, tps + 1, STATE, width), F32),
        vmem((groups, tps, STATE, width), F32),
        vmem((groups, STATE, width), BF16),
        vmem((groups, STATE, width), BF16),
        vmem((groups, STATE, width), BF16),
        vmem((groups, STATE, width), BF16),
        vmem((chunk, width), F32),
        vmem((chunk, width), F32),
        vmem((chunk, chunk), F32),
        vmem((3 * chunk, width), BF16),
        vmem((8, width), F32),
        vmem((length, columns), BF16),
        vmem((groups, tps, chunk, 2 * STATE), BF16),
        vmem((groups, tps, chunk, 2 * STATE), BF16),
        vmem((8, LANES), F32),
        vmem((max(ctxs - 1, 1), 8, LANES), F32),
        dma((groups,)),
        dma((groups,)),
        dma((groups,)),
        dma((groups,)),
        dma((groups, tps)),
        dma((groups, tps)),
        dma((groups, tps)),
        dma((groups, tps)),
        dma((max(ctxs - 1, 1),)),
        dma((max(ctxs - 1, 1),)),
    ]
    whole = pl.BlockSpec(memory_space=pltpu.VMEM)
    upstream, grad_delta, vectors, params = pl.pallas_call(
        functools.partial(kernel, sizes),
        out_shape=(
            jax.ShapeDtypeStruct((length, columns), BF16),
            jax.ShapeDtypeStruct((length, heads), F32),
            jax.ShapeDtypeStruct((chunk, groups * tps * 2 * STATE), F32),
            jax.ShapeDtypeStruct((3, heads), F32),
        ),
        in_specs=[whole] * 8,
        out_specs=(pl.BlockSpec(memory_space=pl.ANY), whole, whole, whole),
        scratch_shapes=scratch,
        compiler_params=pltpu.CompilerParams(
            collective_id=0, has_side_effects=True, vmem_limit_bytes=56 * 1024 * 1024
        ),
    )(
        mixer_input[0],
        write_vectors[0],
        read_vectors[0],
        delta_raw[0],
        log_rates,
        delta_bias,
        skip_gain,
        output_grad[0],
    )
    last = lax.axis_index("section") == sections - 1
    upstream = jnp.where(last, jnp.zeros_like(upstream), upstream)
    return (upstream[None], grad_delta[None], vectors[None], params[None])


def solution(mesh):
    sizes = tuple(mesh.shape[a] for a in ("section", "ctx", "tp"))
    in_specs = (
        P("section", "ctx", "tp"),
        P("section", "ctx", "tp"),
        P("section", "ctx", "tp"),
        P("section", "ctx", "tp"),
        P("section", "tp"),
        P("section", "tp"),
        P("section", "tp"),
        P("section", "ctx", "tp"),
    )
    out_specs = (
        P("section", "ctx", "tp"),
        P("section", "ctx", "tp"),
        P("section", ("ctx", "tp"), None),
        P("section", None, "tp"),
    )
    return jax.shard_map(
        functools.partial(shards, sizes),
        mesh=mesh,
        in_specs=in_specs,
        out_specs=out_specs,
        check_vma=False,
    )
```

profile of v0, /device:TPU:1, one launch (start us, length us, event | category | flops | bytes accessed | tf_op | source)
XLA Modules:
  0.0 53.8 jit_solution(14076734171231165670)
XLA Ops:
  0.6 1.7 %copy.12 = f32[1,512,32]{2,1,0:T(8,128)} copy(f32[1,512,32]{1,2,0:T(8,128)} %param.11) | data formatting | bytes 131072 | tf_op args[3]
  2.3 46.0 %shard_map.111 = (bf16[512,2048]{1,0:T(8,128)(2,1)}, f32[512,32]{1,0:T(8,128)}, f32[128,2048]{1,0:T(8,128)}, f32[3,32]{1,0:T(4,128)}) custom-call(bf16[512,2048]{1,0:T(8,128)(2,1)} %bitcast.10, bf16[512,256]{1,0:T(8,128)(2,1)} %bitcast.14, bf16[512,256]{1,0:T(8,128)(2,1)} %bitcast.15, f32[512,32]{1,0:T(8,128)} %bitcast.12, f32[1,32]{1,0:T(1,128)} %rates_ref.1, ...), custom_call_target="tpu_custom_call" | custom-call | tf_op jit(solution)/shard_map/pallas_call | solution.py:510
  48.3 0.0 copy-start.1
  48.3 0.0 copy-start.2
  48.3 0.0 copy-start
  48.4 3.2 %select_bitcast_fusion = bf16[1,512,2048]{2,1,0:T(8,128)(2,1)} fusion(bf16[512,2048]{1,0:T(8,128)(2,1)} %get-tuple-element.8, pred[]{:T(512)S(6)} %eq.3), kind=kLoop, calls=%fused_computation | loop fusion | flops 1048576 | bytes 4194305 | tf_op jit(solution)/shard_map/broadcast_in_dim | solution.py:536
  51.5 0.0 copy-done.1
  51.5 0.7 %copy.13 = f32[1,512,32]{1,2,0:T(8,128)} copy(f32[1,512,32]{2,1,0:T(8,128)S(1)} %bitcast.16) | data formatting | bytes 131072
  52.3 0.0 copy-done.2
  52.3 0.6 %copy.14 = f32[1,3,32]{2,0,1:T(1,128)} copy(f32[1,3,32]{2,1,0:T(4,128)S(1)} %bitcast.17) | data formatting | bytes 768
  52.8 0.0 copy-done
  52.8 1.0 %copy.16 = f32[1,128,2048]{2,1,0:T(8,128)} copy(f32[1,128,2048]{2,1,0:T(8,128)S(1)} %bitcast.13) | data formatting | bytes 2097152
Async XLA Ops:
  48.3 3.2 %copy-start.1 = (f32[512,32]{1,0:T(8,128)S(1)}, f32[512,32]{1,0:T(8,128)}, u32[]{:S(2)}) copy-start(f32[512,32]{1,0:T(8,128)} %get-tuple-element.9) | copy-start | bytes 196612
  48.3 3.9 %copy-start.2 = (f32[3,32]{1,0:T(4,128)S(1)}, f32[3,32]{1,0:T(4,128)}, u32[]{:S(2)}) copy-start(f32[3,32]{1,0:T(4,128)} %get-tuple-element.11) | copy-start | bytes 1156
  48.3 4.5 %copy-start = (f32[128,2048]{1,0:T(8,128)S(1)}, f32[128,2048]{1,0:T(8,128)}, u32[]{:S(2)}) copy-start(f32[128,2048]{1,0:T(8,128)} %get-tuple-element.10) | copy-start | bytes 3145732
where the time goes:
time: 54 us; the launch traced here: 53.8 us
  Pallas kernels  46 us (85%)
  local copies, waits for them, and re-layouts  3.96 us (7%)
  other arithmetic  3.16 us (6%)
  between operations  0.67 us (1%)
    pallas_call x1, Pallas kernels, shards(): pl.pallas_call(functools.partial(kernel, sizes), out_shape=(jax.ShapeDtyp...  46 us
    unnamed x10, local copies, waits for them, and re-layouts  3.96 us
    broadcast_in_dim x1, other arithmetic, shards(): return (upstream[None], grad_delta[None], vectors[None], params[None])  3.16 us

commit v1 on v0

--- a/solution.py
+++ b/solution.py
@@ -30,6 +30,20 @@
 
 def dot_tn(a, b):
     return lax.dot_general(a, b, (((0,), (0,)), ((), ())), preferred_element_type=F32)
+
+
+def split(a, parts):
+    out = []
+    for _ in range(parts):
+        out.append(a.astype(BF16))
+        a = a - out[-1].astype(F32)
+    return out
+
+
+def dot_exact(a, b):
+    rows = a.shape[0]
+    terms = dot_nn(jnp.concatenate(split(a, 3), axis=0), b)
+    return terms[0:rows] + terms[rows : 2 * rows] + terms[2 * rows : 3 * rows]
 
 
 def kernel(
@@ -49,7 +63,7 @@
     cum,
     cum_rows,
     step_rows,
-    tail,
+    scales,
     decay,
     ratio,
     slope,
@@ -86,7 +100,7 @@
 ):
     sections, ctxs, tps = sizes
     section, ctx, tp = (lax.axis_index(a) for a in ("section", "ctx", "tp"))
-    length, heads = delta_ref.shape
+    heads, length = delta_ref.shape
     groups = w_ref.shape[1] // STATE
     per_group = heads // groups
     width = per_group * HEADDIM
@@ -115,25 +129,35 @@
     up_to = lax.broadcasted_iota(jnp.int32, (chunk, chunk), 0)
     from_ = lax.broadcasted_iota(jnp.int32, (chunk, chunk), 1)
     causal = up_to >= from_
-    lower = causal.astype(F32)
-    upper = (up_to <= from_).astype(F32)
+    lower = causal.astype(BF16)
+    upper = (up_to <= from_).astype(BF16)
     first_half = lax.broadcasted_iota(jnp.int32, (chunk, LANES), 1) < HEADDIM
-    rate = jnp.exp(rates_ref[...])
+    rate = jnp.transpose(jnp.broadcast_to(jnp.exp(rates_ref[...]), (chunk, heads)))
+    bias = jnp.transpose(jnp.broadcast_to(bias_ref[...], (chunk, heads)))
     for k in range(chunks):
         rows = slice(k * chunk, (k + 1) * chunk)
-        z = delta_ref[rows, :] + bias_ref[...]
+        z = delta_ref[:, rows] + bias
         small = jnp.exp(-jnp.abs(z))
         step = jnp.maximum(z, 0.0) + jnp.log1p(small)
         sig = jnp.where(z >= 0, 1.0, small) / (1.0 + small)
         dec = -step * rate
-        decay[rows, :] = dec
-        ratio[rows, :] = jnp.where(step > 1e-37, sig / jnp.maximum(step, 1e-37), 1.0)
-        slope[rows, :] = sig * rate
-        run = dot_nn(lower, dec * LOG2E, HIGHEST)
-        cum[rows, :] = run
-        tail[rows, :] = jnp.exp2(run[chunk - 1 : chunk, :] - run) * step
-        cum_rows[:, rows] = jnp.transpose(run)
-        step_rows[:, rows] = jnp.transpose(step)
+        decay[:, rows] = dec
+        ratio[:, rows] = jnp.where(step > 1e-37, sig / jnp.maximum(step, 1e-37), 1.0)
+        slope[:, rows] = sig * rate
+        run = dot_exact(dec * LOG2E, upper)
+        cum[rows, :] = jnp.transpose(run)
+        cum_rows[:, rows] = run
+        step_rows[:, rows] = step
+        lead = split(jnp.exp2(run), 2)
+        tail = split(jnp.exp2(run[:, chunk - 1 : chunk] - run) * step, 2)
+        for g in range(groups):
+            own = slice(g * per_group, (g + 1) * per_group)
+            scales[g, 0, :, rows] = jnp.concatenate([lead[0][own], lead[1][own]], axis=0)
+            scales[g, 1, :, rows] = jnp.concatenate([tail[0][own], tail[1][own]], axis=0)
+    head_of = lax.broadcasted_iota(jnp.int32, (2 * per_group, width), 1) // HEADDIM
+    row_of = lax.broadcasted_iota(jnp.int32, (2 * per_group, width), 0)
+    both = (head_of == lax.rem(row_of, per_group)).astype(BF16)
+    gather = both[0:per_group]
 
     def entered():
         peers = (ctxs - 1) + (tps - 1)
@@ -144,28 +168,17 @@
         start = g * width + j * LANES
         return slice(start, start + LANES)
 
-    def spread(ref, rows, head):
-        both = ref[rows, head : head + 2]
-        return jnp.where(
-            first_half,
-            jnp.broadcast_to(both[:, 0:1], (chunk, LANES)),
-            jnp.broadcast_to(both[:, 1:2], (chunk, LANES)),
-        )
-
     def increments(g):
         def one(k, carry):
             rows = pl.ds(pl.multiple_of(k * chunk, chunk), chunk)
-            for j in range(pairs):
-                at = columns(g, j)
-                head = g * per_group + 2 * j
-                lead_pair = jnp.exp2(spread(cum, rows, head))
-                tail_pair = spread(tail, rows, head)
-                lead_wide[rows, at] = lead_pair
-                tail_wide[rows, at] = tail_pair
-                lead_dy[rows, at] = (lead_pair * dy_ref[rows, at].astype(F32)).astype(BF16)
-                tail_x[rows, at] = (tail_pair * x_ref[rows, at].astype(F32)).astype(BF16)
             group_at = slice(g * width, (g + 1) * width)
             vec_at = slice(g * STATE, (g + 1) * STATE)
+            lead_all = dot_tn(scales[g, 0, :, rows], both)
+            tail_all = dot_tn(scales[g, 1, :, rows], both)
+            lead_wide[rows, group_at] = lead_all
+            tail_wide[rows, group_at] = tail_all
+            lead_dy[rows, group_at] = (lead_all * dy_ref[rows, group_at].astype(F32)).astype(BF16)
+            tail_x[rows, group_at] = (tail_all * x_ref[rows, group_at].astype(F32)).astype(BF16)
             states[g, k] = dot_tn(w_ref[rows, vec_at], tail_x[rows, group_at])
             exits[g, k] = dot_tn(r_ref[rows, vec_at], lead_dy[rows, group_at])
             return carry
@@ -288,11 +301,7 @@
     def quadratic(g):
         vec_at = slice(g * STATE, (g + 1) * STATE)
         group_at = slice(g * width, (g + 1) * width)
-        gather = (
-            lax.broadcasted_iota(jnp.int32, (width, heads), 0) // HEADDIM + g * per_group
-            == lax.broadcasted_iota(jnp.int32, (width, heads), 1)
-        ).astype(F32)
-        gather_short = gather.astype(BF16)
+        own = slice(g * per_group, (g + 1) * per_group)
 
         def one(k, carry):
             rows = pl.ds(pl.multiple_of(k * chunk, chunk), chunk)
@@ -348,9 +357,11 @@
             def _():
                 dx_copy(g, k).start()
 
-            inner = jnp.where(causal, da[...], 0.0).astype(BF16)
-            dw = dot_tn(inner, r) + dot_nt(tail_x[rows, group_at], exit_)
-            dr = dot_nn(inner, w) + dot_nt(lead_dy[rows, group_at], state)
+            inner = split(jnp.where(causal, da[...], 0.0), 2)
+            dw = dot_tn(jnp.concatenate(inner, axis=0), jnp.concatenate([r, r], axis=0))
+            dr = dot_nn(jnp.concatenate(inner, axis=1), jnp.concatenate([w, w], axis=0))
+            dw = dw + dot_nt(tail_x[rows, group_at], exit_)
+            dr = dr + dot_nt(lead_dy[rows, group_at], state)
 
             @pl.when(tp == k)
             def _():
@@ -363,20 +374,16 @@
                 vec_out[g, k, :, STATE : 2 * STATE] = dr.astype(BF16)
                 vec_copy(g, k).start()
 
-            sums = dot_nn(pieces[...], gather_short)
-            ends = dot_nn(edge[...], gather, HIGHEST)
-            difference = sums[0:chunk] + sums[chunk : 2 * chunk]
-            decay_grad = dot_nn(upper, difference, HIGHEST) + ends[0:1]
-            grad = sums[2 * chunk : 3 * chunk] * ratio[rows, :] - decay_grad * slope[rows, :]
-            mine = lax.broadcasted_iota(jnp.int32, (chunk, heads), 1) // per_group == g
-            grad = jnp.where(mine, grad, 0.0)
-            if g == 0:
-                gdelta_ref[rows, :] = grad
-            else:
-                gdelta_ref[rows, :] += grad
-            part[0:1, 0:heads] += jnp.sum(decay_grad * decay[rows, :], axis=0, keepdims=True)
-            part[1:2, 0:heads] += jnp.sum(grad, axis=0, keepdims=True)
-            part[2:3, 0:heads] += ends[1:2]
+            sums = dot_nt(gather, pieces[...])
+            edges = split(edge[...], 2)
+            ends = dot_nt(gather, edges[0]) + dot_nt(gather, edges[1])
+            difference = sums[:, 0:chunk] + sums[:, chunk : 2 * chunk]
+            decay_grad = dot_exact(difference, lower) + ends[:, 0:1]
+            grad = sums[:, 2 * chunk :] * ratio[own, rows] - decay_grad * slope[own, rows]
+            gdelta_ref[own, rows] = grad
+            part[own, 0:1] += jnp.sum(decay_grad * decay[own, rows], axis=1, keepdims=True)
+            part[own, 1:2] += jnp.sum(grad, axis=1, keepdims=True)
+            part[own, 2:3] += ends[:, 1:2]
             return carry
 
         lax.fori_loop(0, chunks, one, 0)
@@ -426,12 +433,12 @@
         lax.fori_loop(0, tps, vectors, 0)
         for k in range(tps):
             start = (k * groups + g) * 2 * STATE
-            vec_ref[:, start : start + 2 * STATE] = vec_in[g, k].astype(F32)
+            vec_ref[:, start : start + 2 * STATE] = vec_in[g, k]
     result = part[...]
     for hop in range(1, ctxs):
         part_copy(hop).wait()
         result = result + parts[hop - 1]
-    params_ref[...] = result[0:3, 0:heads]
+    params_ref[...] = jnp.transpose(result)[0:8]
     for g in range(groups):
 
         def moved(k, carry):
@@ -446,6 +453,14 @@
             return carry
 
         lax.fori_loop(0, chunks, moved, 0)
+
+
+def finish(sections, up_ref, gdelta_ref, vec_ref, params_ref, up_out, gdelta_out, vec_out, out):
+    last = lax.axis_index("section") == sections - 1
+    up_out[...] = jnp.where(last, jnp.zeros_like(up_ref[...]), up_ref[...])
+    gdelta_out[...] = gdelta_ref[...]
+    vec_out[...] = vec_ref[...].astype(F32)
+    out[...] = params_ref[0:3]
 
 
 def shards(
@@ -471,10 +486,10 @@
         vmem((length, heads), F32),
         vmem((heads, length), F32),
         vmem((heads, length), F32),
-        vmem((length, heads), F32),
-        vmem((length, heads), F32),
-        vmem((length, heads), F32),
-        vmem((length, heads), F32),
+        vmem((groups, 2, 2 * heads // groups, length), BF16),
+        vmem((heads, length), F32),
+        vmem((heads, length), F32),
+        vmem((heads, length), F32),
         vmem((length, columns), F32),
         vmem((length, columns), F32),
         vmem((length, columns), BF16),
@@ -493,8 +508,8 @@
         vmem((length, columns), BF16),
         vmem((groups, tps, chunk, 2 * STATE), BF16),
         vmem((groups, tps, chunk, 2 * STATE), BF16),
-        vmem((8, LANES), F32),
-        vmem((max(ctxs - 1, 1), 8, LANES), F32),
+        vmem((heads, LANES), F32),
+        vmem((max(ctxs - 1, 1), heads, LANES), F32),
         dma((groups,)),
         dma((groups,)),
         dma((groups,)),
@@ -511,9 +526,9 @@
         functools.partial(kernel, sizes),
         out_shape=(
             jax.ShapeDtypeStruct((length, columns), BF16),
-            jax.ShapeDtypeStruct((length, heads), F32),
-            jax.ShapeDtypeStruct((chunk, groups * tps * 2 * STATE), F32),
-            jax.ShapeDtypeStruct((3, heads), F32),
+            jax.ShapeDtypeStruct((heads, length), F32),
+            jax.ShapeDtypeStruct((chunk, groups * tps * 2 * STATE), BF16),
+            jax.ShapeDtypeStruct((8, heads), F32),
         ),
         in_specs=[whole] * 8,
         out_specs=(pl.BlockSpec(memory_space=pl.ANY), whole, whole, whole),
@@ -525,15 +540,32 @@
         mixer_input[0],
         write_vectors[0],
         read_vectors[0],
-        delta_raw[0],
+        delta_raw[0].T,
         log_rates,
         delta_bias,
         skip_gain,
         output_grad[0],
     )
-    last = lax.axis_index("section") == sections - 1
-    upstream = jnp.where(last, jnp.zeros_like(upstream), upstream)
-    return (upstream[None], grad_delta[None], vectors[None], params[None])
+    steps = 4
+    rows, across = length // steps, vectors.shape[1] // steps
+    specs = [
+        pl.BlockSpec((rows, columns), lambda i: (i, 0)),
+        pl.BlockSpec((heads, length), lambda i: (0, 0)),
+        pl.BlockSpec((chunk, across), lambda i: (0, i)),
+    ]
+    upstream, grad_delta, vectors, params = pl.pallas_call(
+        functools.partial(finish, sections),
+        grid=(steps,),
+        out_shape=(
+            jax.ShapeDtypeStruct((length, columns), BF16),
+            jax.ShapeDtypeStruct((heads, length), F32),
+            jax.ShapeDtypeStruct(vectors.shape, F32),
+            jax.ShapeDtypeStruct((3, heads), F32),
+        ),
+        in_specs=specs + [pl.BlockSpec((8, heads), lambda i: (0, 0))],
+        out_specs=tuple(specs + [pl.BlockSpec((3, heads), lambda i: (0, 0))]),
+    )(upstream, grad_delta, vectors, params)
+    return (upstream[None], grad_delta.T[None], vectors[None], params[None])
 
 
 def solution(mesh):

time: 54 us -> 50.9 us (0.943)
  other arithmetic: 3.16 us -> 0 us
  Pallas kernels: 46 us -> 48.9 us
  local copies, waits for them, and re-layouts: 3.96 us -> 1.24 us
    pallas_call x0 -> x1, Pallas kernels: none -> 4.1 us  [shards(): pl.pallas_call(functools.partial(finish, sections), grid=(steps,), out_sh...]
    broadcast_in_dim x1 -> x0, other arithmetic: 3.16 us -> none  [shards(): return (upstream[None], grad_delta[None], vectors[None], params[None])]
    unnamed x10 -> x1, local copies, waits for them, and re-layouts: 3.96 us -> 1.24 us
    pallas_call x1, Pallas kernels: 46 us -> 44.7 us  [shards(): pl.pallas_call(functools.partial(kernel, sizes), out_shape=(jax.ShapeDtyp...]
where the time goes in v1:
time: 50.9 us; the launch traced here: 50.7 us
  Pallas kernels  48.9 us (96%)
  local copies, waits for them, and re-layouts  1.24 us (2%)
  between operations  0.64 us (1%)
    pallas_call x1, Pallas kernels, shards(): pl.pallas_call(functools.partial(kernel, sizes), out_shape=(jax.ShapeDtyp...  44.7 us
    pallas_call x1, Pallas kernels, shards(): pl.pallas_call(functools.partial(finish, sections), grid=(steps,), out_sh...  4.1 us
    unnamed x1, local copies, waits for them, and re-layouts  1.24 us

profile of v1, /device:TPU:1, one launch (start us, length us, event | category | flops | bytes accessed | tf_op | source)
XLA Modules:
  0.0 50.7 jit_solution(8429900854574592851)
XLA Ops:
  0.6 44.7 %shard_map.111 = (bf16[512,2048]{1,0:T(8,128)(2,1)}, f32[32,512]{1,0:T(8,128)}, bf16[128,2048]{1,0:T(8,128)(2,1)}, f32[8,32]{1,0:T(8,128)}) custom-call(bf16[512,2048]{1,0:T(8,128)(2,1)} %bitcast.13, bf16[512,256]{1,0:T(8,128)(2,1)} %bitcast.15, bf16[512,256]{1,0:T(8,128)(2,1)} %bitcast.16, f32[32,512]{1,0:T(8,128)} %bitcast.17, f32[1,32]{1,0:T(1,128)} %rates_ref.1, ...), custom_call_target="tpu_custom_call" | custom-call | tf_op jit(solution)/shard_map/pallas_call | solution.py:525
  45.4 4.1 %shard_map.112 = (bf16[512,2048]{1,0:T(8,128)(2,1)}, f32[32,512]{1,0:T(8,128)}, f32[128,2048]{1,0:T(8,128)}, f32[3,32]{1,0:T(4,128)}) custom-call(bf16[512,2048]{1,0:T(8,128)(2,1)} %get-tuple-element.12.up_ref, f32[32,512]{1,0:T(8,128)} %get-tuple-element.13.gdelta_ref, bf16[128,2048]{1,0:T(8,128)(2,1)} %get-tuple-element.14.vec_ref, ...), custom_call_target="tpu_custom_call" | custom-call | tf_op jit(solution)/shard_map/pallas_call | solution.py:556
  49.5 1.2 %copy.12 = f32[1,3,32]{2,0,1:T(1,128)} copy(f32[1,3,32]{2,1,0:T(4,128)} %bitcast.18) | data formatting | bytes 768

commit v2 on v1

--- a/solution.py
+++ b/solution.py
@@ -48,18 +48,20 @@
 
 def kernel(
     sizes,
-    x_ref,
+    x_hbm,
     w_ref,
     r_ref,
     delta_ref,
     rates_ref,
     bias_ref,
     skip_ref,
-    dy_ref,
+    dy_hbm,
     up_ref,
     gdelta_ref,
     vec_ref,
     params_ref,
+    x_ref,
+    dy_ref,
     cum,
     cum_rows,
     step_rows,
@@ -87,6 +89,7 @@
     vec_in,
     part,
     parts,
+    loads,
     s_send,
     s_recv,
     e_send,
@@ -107,6 +110,17 @@
     chunk = length // tps
     chunks = tps
     pairs = width // LANES
+
+    def load(g):
+        at = pl.ds(g * width, width)
+        return (
+            pltpu.make_async_copy(x_hbm.at[:, at], x_ref.at[:, at], loads.at[0, g]),
+            pltpu.make_async_copy(dy_hbm.at[:, at], dy_ref.at[:, at], loads.at[1, g]),
+        )
+
+    for g in range(groups):
+        for copy in load(g):
+            copy.start()
 
     barrier = pltpu.get_barrier_semaphore()
     for hop in range(1, ctxs):
@@ -169,6 +183,9 @@
         return slice(start, start + LANES)
 
     def increments(g):
+        for copy in load(g):
+            copy.wait()
+
         def one(k, carry):
             rows = pl.ds(pl.multiple_of(k * chunk, chunk), chunk)
             group_at = slice(g * width, (g + 1) * width)
@@ -177,10 +194,13 @@
             tail_all = dot_tn(scales[g, 1, :, rows], both)
             lead_wide[rows, group_at] = lead_all
             tail_wide[rows, group_at] = tail_all
-            lead_dy[rows, group_at] = (lead_all * dy_ref[rows, group_at].astype(F32)).astype(BF16)
-            tail_x[rows, group_at] = (tail_all * x_ref[rows, group_at].astype(F32)).astype(BF16)
-            states[g, k] = dot_tn(w_ref[rows, vec_at], tail_x[rows, group_at])
-            exits[g, k] = dot_tn(r_ref[rows, vec_at], lead_dy[rows, group_at])
+            w, r = w_ref[rows, vec_at], r_ref[rows, vec_at]
+            later = split(tail_all * x_ref[rows, group_at].astype(F32), 2)
+            tail_x[rows, group_at] = later[0]
+            states[g, k] = dot_tn(jnp.concatenate([w, w], axis=0), jnp.concatenate(later, axis=0))
+            later = split(lead_all * dy_ref[rows, group_at].astype(F32), 2)
+            lead_dy[rows, group_at] = later[0]
+            exits[g, k] = dot_tn(jnp.concatenate([r, r], axis=0), jnp.concatenate(later, axis=0))
             return carry
 
         lax.fori_loop(0, chunks, one, 0)
@@ -266,14 +286,14 @@
             def _():
                 exit_copy(g).start()
 
-    def dx_copy(g, k):
+    def dx_copy(g, k, half):
         rows = pl.ds(pl.multiple_of(k * chunk, chunk), chunk)
-        at = pl.ds(g * width, width)
+        at = pl.ds(g * width + half * (width // 2), width // 2)
         return pltpu.make_async_remote_copy(
             src_ref=dx.at[rows, at],
             dst_ref=up_ref.at[rows, at],
-            send_sem=x_send.at[g, k],
-            recv_sem=x_recv.at[g, k],
+            send_sem=x_send.at[g, k, half],
+            recv_sem=x_recv.at[g, k, half],
             device_id={"section": jnp.maximum(section - 1, 0)},
             device_id_type=MESH,
         )
@@ -308,9 +328,13 @@
             w, r = w_ref[rows, vec_at], r_ref[rows, vec_at]
             scores = jnp.where(causal, dot_nt(r, w), 0.0)
             da[...] = jnp.zeros_like(da)
-            state, exit_ = states[g, k].astype(BF16), exits[g, k].astype(BF16)
-            read_state[...] = dot_nn(r, state)
-            write_exit[...] = dot_nn(w, exit_)
+            state, exit_ = split(states[g, k], 2), split(exits[g, k], 2)
+            read_state[...] = dot_nn(
+                jnp.concatenate([r, r], axis=1), jnp.concatenate(state, axis=0)
+            )
+            write_exit[...] = dot_nn(
+                jnp.concatenate([w, w], axis=1), jnp.concatenate(exit_, axis=0)
+            )
             edge[0:1, :] = jnp.sum(exits[g, k] * states[g, k + 1], axis=0, keepdims=True)
             for j in range(pairs):
                 at = columns(g, j)
@@ -344,7 +368,9 @@
                 high = rest.astype(BF16)
                 pieces[0:chunk, here] = high
                 pieces[chunk : 2 * chunk, here] = (rest - high.astype(F32)).astype(BF16)
-                pieces[2 * chunk : 3 * chunk, here] = column.astype(BF16)
+                high = column.astype(BF16)
+                pieces[2 * chunk : 3 * chunk, here] = high
+                pieces[3 * chunk : 4 * chunk, here] = (column - high.astype(F32)).astype(BF16)
                 edge[1:2, here] = jnp.sum(x32 * dy32, axis=0, keepdims=True)
                 gain = jnp.where(
                     first_half[0:1],
@@ -352,16 +378,19 @@
                     jnp.broadcast_to(skip_ref[:, head + 1 : head + 2], (1, LANES)),
                 )
                 dx[rows, at] = (dxs + gain * dy32).astype(BF16)
-
-            @pl.when(section > 0)
-            def _():
-                dx_copy(g, k).start()
+                if (j + 1) % (pairs // 2) == 0:
+
+                    @pl.when(section > 0)
+                    def _(half=j // (pairs // 2)):
+                        dx_copy(g, k, half).start()
+
 
             inner = split(jnp.where(causal, da[...], 0.0), 2)
             dw = dot_tn(jnp.concatenate(inner, axis=0), jnp.concatenate([r, r], axis=0))
             dr = dot_nn(jnp.concatenate(inner, axis=1), jnp.concatenate([w, w], axis=0))
-            dw = dw + dot_nt(tail_x[rows, group_at], exit_)
-            dr = dr + dot_nt(lead_dy[rows, group_at], state)
+            for i in range(2):
+                dw = dw + dot_nt(tail_x[rows, group_at], exit_[i])
+                dr = dr + dot_nt(lead_dy[rows, group_at], state[i])
 
             @pl.when(tp == k)
             def _():
@@ -379,7 +408,8 @@
             ends = dot_nt(gather, edges[0]) + dot_nt(gather, edges[1])
             difference = sums[:, 0:chunk] + sums[:, chunk : 2 * chunk]
             decay_grad = dot_exact(difference, lower) + ends[:, 0:1]
-            grad = sums[:, 2 * chunk :] * ratio[own, rows] - decay_grad * slope[own, rows]
+            direct = sums[:, 2 * chunk : 3 * chunk] + sums[:, 3 * chunk :]
+            grad = direct * ratio[own, rows] - decay_grad * slope[own, rows]
             gdelta_ref[own, rows] = grad
             part[own, 0:1] += jnp.sum(decay_grad * decay[own, rows], axis=1, keepdims=True)
             part[own, 1:2] += jnp.sum(grad, axis=1, keepdims=True)
@@ -390,11 +420,30 @@
 
     part[...] = jnp.zeros_like(part)
     edge[...] = jnp.zeros_like(edge)
+    early = lax.rem(section, 2) == 0
     for g in range(groups):
         increments(g)
         if g == 0:
             entered()
-        begin(g)
+
+            @pl.when(early)
+            def _():
+                begin(0)
+
+        else:
+            if g == 1:
+
+                @pl.when(jnp.logical_not(early))
+                def _():
+                    begin(0)
+
+            begin(g)
+    if groups == 1:
+
+        @pl.when(jnp.logical_not(early))
+        def _():
+            begin(0)
+
     for g in range(groups):
         link(g)
         quadratic(g)
@@ -444,11 +493,13 @@
         def moved(k, carry):
             @pl.when(section > 0)
             def _():
-                dx_copy(g, k).wait_send()
+                for half in range(2):
+                    dx_copy(g, k, half).wait_send()
 
             @pl.when(section < sections - 1)
             def _():
-                dx_copy(g, k).wait_recv()
+                for half in range(2):
+                    dx_copy(g, k, half).wait_recv()
 
             return carry
 
@@ -460,7 +511,8 @@
     up_out[...] = jnp.where(last, jnp.zeros_like(up_ref[...]), up_ref[...])
     gdelta_out[...] = gdelta_ref[...]
     vec_out[...] = vec_ref[...].astype(F32)
-    out[...] = params_ref[0:3]
+    for i in range(3):
+        out[i] = params_ref[i : i + 1]
 
 
 def shards(
@@ -483,6 +535,8 @@
     dma = pltpu.SemaphoreType.DMA
     vmem = pltpu.VMEM
     scratch = [
+        vmem((length, columns), BF16),
+        vmem((length, columns), BF16),
         vmem((length, heads), F32),
         vmem((heads, length), F32),
         vmem((heads, length), F32),
@@ -503,25 +557,27 @@
         vmem((chunk, width), F32),
         vmem((chunk, width), F32),
         vmem((chunk, chunk), F32),
-        vmem((3 * chunk, width), BF16),
+        vmem((4 * chunk, width), BF16),
         vmem((8, width), F32),
         vmem((length, columns), BF16),
         vmem((groups, tps, chunk, 2 * STATE), BF16),
         vmem((groups, tps, chunk, 2 * STATE), BF16),
         vmem((heads, LANES), F32),
         vmem((max(ctxs - 1, 1), heads, LANES), F32),
+        dma((2, groups)),
         dma((groups,)),
         dma((groups,)),
         dma((groups,)),
         dma((groups,)),
-        dma((groups, tps)),
-        dma((groups, tps)),
+        dma((groups, tps, 2)),
+        dma((groups, tps, 2)),
         dma((groups, tps)),
         dma((groups, tps)),
         dma((max(ctxs - 1, 1),)),
         dma((max(ctxs - 1, 1),)),
     ]
     whole = pl.BlockSpec(memory_space=pltpu.VMEM)
+    far = pl.BlockSpec(memory_space=pl.ANY)
     upstream, grad_delta, vectors, params = pl.pallas_call(
         functools.partial(kernel, sizes),
         out_shape=(
@@ -530,8 +586,8 @@
             jax.ShapeDtypeStruct((chunk, groups * tps * 2 * STATE), BF16),
             jax.ShapeDtypeStruct((8, heads), F32),
         ),
-        in_specs=[whole] * 8,
-        out_specs=(pl.BlockSpec(memory_space=pl.ANY), whole, whole, whole),
+        in_specs=[far] + [whole] * 6 + [far],
+        out_specs=(far, whole, whole, whole),
         scratch_shapes=scratch,
         compiler_params=pltpu.CompilerParams(
             collective_id=0, has_side_effects=True, vmem_limit_bytes=56 * 1024 * 1024
@@ -560,12 +616,12 @@
             jax.ShapeDtypeStruct((length, columns), BF16),
             jax.ShapeDtypeStruct((heads, length), F32),
             jax.ShapeDtypeStruct(vectors.shape, F32),
-            jax.ShapeDtypeStruct((3, heads), F32),
+            jax.ShapeDtypeStruct((3, 1, heads), F32),
         ),
         in_specs=specs + [pl.BlockSpec((8, heads), lambda i: (0, 0))],
-        out_specs=tuple(specs + [pl.BlockSpec((3, heads), lambda i: (0, 0))]),
+        out_specs=tuple(specs + [pl.BlockSpec((3, 1, heads), lambda i: (0, 0, 0))]),
     )(upstream, grad_delta, vectors, params)
-    return (upstream[None], grad_delta.T[None], vectors[None], params[None])
+    return (upstream[None], grad_delta.T[None], vectors[None], params.transpose(1, 0, 2))
 
 
 def solution(mesh):

time: 50.9 us -> 47.6 us (0.935); the launches traced: 50.7 us -> 46.7 us
  Pallas kernels: 48.9 us -> 46.1 us
  local copies, waits for them, and re-layouts: 1.24 us -> 0 us
    pallas_call x1, Pallas kernels: 44.7 us -> 42 us  [shards(): pl.pallas_call(functools.partial(kernel, sizes), out_shape=(jax.ShapeDtyp...]
    unnamed x1 -> x0, local copies, waits for them, and re-layouts: 1.24 us -> none
where the time goes in v2:
time: 47.6 us; the launch traced here: 46.7 us
  Pallas kernels  46.1 us (97%)
  between operations  0.64 us (1%)
    pallas_call x1, Pallas kernels, shards(): pl.pallas_call(functools.partial(kernel, sizes), out_shape=(jax.ShapeDtyp...  42 us
    pallas_call x1, Pallas kernels, shards(): pl.pallas_call(functools.partial(finish, sections), grid=(steps,), out_sh...  4.1 us

profile of v2, /device:TPU:1, one launch (start us, length us, event | category | flops | bytes accessed | tf_op | source)
XLA Modules:
  0.0 46.7 jit_solution(17158065076529826015)
XLA Ops:
  0.6 42.0 %shard_map.111 = (bf16[512,2048]{1,0:T(8,128)(2,1)}, f32[32,512]{1,0:T(8,128)}, bf16[128,2048]{1,0:T(8,128)(2,1)}, f32[8,32]{1,0:T(8,128)}) custom-call(bf16[512,2048]{1,0:T(8,128)(2,1)} %bitcast.13, bf16[512,256]{1,0:T(8,128)(2,1)} %bitcast.15, bf16[512,256]{1,0:T(8,128)(2,1)} %bitcast.16, f32[32,512]{1,0:T(8,128)} %bitcast.17, f32[1,32]{1,0:T(1,128)} %rates_ref.1, ...), custom_call_target="tpu_custom_call" | custom-call | tf_op jit(solution)/shard_map/pallas_call | solution.py:581
  42.6 4.1 %shard_map.112 = (bf16[512,2048]{1,0:T(8,128)(2,1)}, f32[32,512]{1,0:T(8,128)}, f32[128,2048]{1,0:T(8,128)}, f32[3,1,32]{2,1,0:T(1,128)}) custom-call(bf16[512,2048]{1,0:T(8,128)(2,1)} %get-tuple-element.12.up_ref, f32[32,512]{1,0:T(8,128)} %get-tuple-element.13.gdelta_ref, bf16[128,2048]{1,0:T(8,128)(2,1)} %get-tuple-element.14.vec_ref, ...), custom_call_target="tpu_custom_call" | custom-call | tf_op jit(solution)/shard_map/pallas_call | solution.py:612
